TPU v7x, 32 devices: a whole 2x2x4 slice. The times are simulated.
32 devices in a mesh: box: 8 (over y, x, core), grp: 4 (over z).
Axes of the slice: x: 2, y: 2, z: 4, core: 2. Of those that a mesh axis runs over, the one named last changes fastest.
Arguments:
- impedance: bfloat16 [2, 8, 1, 2048, 2048], P(None, 'box', None, None, 'grp'), may hold values from -3 to 3
- face_order: int32 [8, 1, 16], replicated, may hold values from 0 to 15, each once within a row
Outputs:
- merged: bfloat16 [2, 8, 1, 4096, 2048], P(None, 'box', None, None, 'grp')
Inputs may be any that keep to these rules, and one draw needn't show every extreme that they name: `face_order`: each row lists the 16 face blocks of one box once; its first 3 entries are the blocks on the face shared with the sibling, the k-th facing the sibling's k-th.
All inputs are finite; a program needn't handle non-finite values.
Results may differ from a plain program's by a relative error of at most 0.0035.
Values may be sent and summed in bfloat16 or wider, within the bound.
A program may use at most 64 MiB of HBM per device.

v0:
```python
import functools

import jax
import jax.numpy as jnp
from jax import lax
from jax.experimental import pallas as pl
from jax.experimental.pallas import tpu as pltpu
from jax.sharding import PartitionSpec as P

BLK = 128
MB = 3
NS_STEPS = 2
ROWS = 64
LAG = 2
MESH_ID = pl.DeviceIdType.MESH
BF16 = jnp.bfloat16
F32 = jnp.float32


def pick_kernel(order_ref, own_ref, mine_ref):
    base = lax.axis_index("box") * (own_ref.shape[1] // BLK)
    blocks = own_ref.shape[2] // BLK
    first = lax.axis_index("grp") * blocks

    def body(block, carry):
        row = pl.multiple_of(order_ref[base + block] * BLK, BLK)
        for k in range(MB):
            local = order_ref[base + k] - first
            held = jnp.logical_and(local >= 0, local < blocks).astype(F32).astype(BF16)
            col = pl.multiple_of(jnp.clip(local, 0, blocks - 1) * BLK, BLK)
            for part in range(2):
                piece = own_ref[part, pl.ds(row, BLK), pl.ds(col, BLK)]
                mine_ref[pl.ds(block * BLK, BLK), pl.ds((part * MB + k) * BLK, BLK)] = piece * held
        return carry

    lax.fori_loop(0, own_ref.shape[1] // BLK, body, 0)


def gather_kernel(
    n, mine_ref, zb_ref, zs_ref, buf_l, buf_r, out_r, out_l,
    send_r, recv_l, send_l, recv_r, send_t, recv_t,
):
    box = lax.axis_index("box")
    grp = lax.axis_index("grp")
    twin = box + 1 - 2 * lax.rem(box, 2)
    chunks = buf_l.shape[0]
    has_left = grp > 0
    has_right = grp < n - 1

    barrier = pltpu.get_barrier_semaphore()
    pl.semaphore_signal(barrier, inc=1, device_id={"box": twin}, device_id_type=MESH_ID)

    @pl.when(has_left)
    def _():
        pl.semaphore_signal(barrier, inc=1, device_id={"grp": grp - 1}, device_id_type=MESH_ID)

    @pl.when(has_right)
    def _():
        pl.semaphore_signal(barrier, inc=1, device_id={"grp": grp + 1}, device_id_type=MESH_ID)

    pl.semaphore_wait(barrier, 1 + has_left.astype(jnp.int32) + has_right.astype(jnp.int32))

    def to_right(c):
        return pltpu.make_async_remote_copy(
            src_ref=out_r.at[c], dst_ref=buf_l.at[c], send_sem=send_r.at[c], recv_sem=recv_l.at[c],
            device_id={"grp": grp + 1}, device_id_type=MESH_ID,
        )

    def to_left(c):
        return pltpu.make_async_remote_copy(
            src_ref=out_l.at[c], dst_ref=buf_r.at[c], send_sem=send_l.at[c], recv_sem=recv_r.at[c],
            device_id={"grp": grp - 1}, device_id_type=MESH_ID,
        )

    def to_twin(c):
        rows = pl.ds(c * ROWS, ROWS)
        return pltpu.make_async_remote_copy(
            src_ref=zb_ref.at[rows], dst_ref=zs_ref.at[rows], send_sem=send_t.at[c], recv_sem=recv_t.at[c],
            device_id={"box": twin}, device_id_type=MESH_ID,
        )

    def mine(c):
        return mine_ref[pl.ds(pl.multiple_of(c * ROWS, ROWS), ROWS), :]

    def left_step(c):
        @pl.when(has_left)
        def _():
            to_right(c).wait_recv()

        @pl.when(jnp.logical_not(has_left))
        def _():
            buf_l[c] = jnp.zeros(buf_l.shape[1:], BF16)

        out_r[c] = mine(c) + buf_l[c]

        @pl.when(has_right)
        def _():
            to_right(c).start()

    def right_step(c):
        @pl.when(has_right)
        def _():
            to_left(c).wait_recv()

        @pl.when(jnp.logical_not(has_right))
        def _():
            buf_r[c] = jnp.zeros(buf_r.shape[1:], BF16)

        out_l[c] = mine(c) + buf_r[c]

        @pl.when(has_left)
        def _():
            to_left(c).start()

    def full_step(c):
        zb_ref[pl.ds(c * ROWS, ROWS), :] = out_r[c] + buf_r[c]
        to_twin(c).start()

    lag_l = LAG * grp
    lag_r = LAG * (n - 1 - grp)
    lag_f = jnp.maximum(lag_l, lag_r)

    def tick(t, carry):
        for lag, step in ((lag_l, left_step), (lag_r, right_step), (lag_f, full_step)):
            c = t - lag

            @pl.when(jnp.logical_and(c >= 0, c < chunks))
            def _():
                step(c)

        return carry

    lax.fori_loop(0, chunks + LAG * (n - 1), tick, 0)

    def drain(c, carry):
        @pl.when(has_right)
        def _():
            to_right(c).wait_send()

        @pl.when(has_left)
        def _():
            to_left(c).wait_send()

        to_twin(c).wait_send()
        to_twin(c).wait_recv()
        return carry

    lax.fori_loop(0, chunks, drain, 0)


def as_right_operand(pair):
    real, imag = pair
    return jnp.concatenate(
        [jnp.concatenate([real, imag], axis=1), jnp.concatenate([-imag, real], axis=1)], axis=0
    )


def product_kernel(rows, order_ref, own_ref, zb_ref, zs_ref, ext_ref, out_ref, rhs, lo, base, held, sems):
    box = lax.axis_index("box")
    parity = lax.rem(box, 2)
    twin = box + 1 - 2 * parity
    points, width = own_ref.shape[1], own_ref.shape[2]
    face_blocks = points // BLK
    iface = MB * BLK
    coupling_sq = 1.0 / points
    coupling = points ** (-0.5)
    ext = ext_ref[...]

    def put(dst, pair):
        real, imag = pair
        dst[pl.ds(0, iface), pl.ds(0, width)] = real
        dst[pl.ds(0, iface), pl.ds(width, width)] = imag
        dst[pl.ds(iface, iface), pl.ds(0, width)] = -imag
        dst[pl.ds(iface, iface), pl.ds(width, width)] = real

    def split(value):
        high = value.astype(BF16)
        low = (value - high.astype(F32)).astype(BF16)
        put(rhs.at[0], (high[:, :width], high[:, width:]))
        put(lo, (low[:, :width], low[:, width:]))

    def apply(z_ref):
        left = z_ref[pl.ds(0, iface), :]
        return jnp.dot(left, rhs[0], preferred_element_type=F32) + jnp.dot(
            left, lo[...], preferred_element_type=F32
        )

    for k in range(MB):
        row = pl.multiple_of(order_ref[box * face_blocks + k] * BLK, BLK)
        for part in range(2):
            base[pl.ds(k * BLK, BLK), pl.ds(part * width, width)] = (
                own_ref[part, pl.ds(row, BLK), :].astype(F32) * ext
            )
    split(base[...])
    response = None
    for _ in range(2**NS_STEPS - 1):
        split(apply(zs_ref))
        response = base[...] + coupling_sq * apply(zb_ref)
        split(response)
    echoed = apply(zs_ref).astype(BF16)
    response = response.astype(BF16)
    put(rhs.at[0], (echoed[:, :width], echoed[:, width:]))
    put(rhs.at[1], (response[:, :width], response[:, width:]))

    per_step = rows // BLK
    steps = points // rows

    def copy_out(slot, half, order_base, block):
        row = half * points + order_ref[order_base + block] * BLK
        return pltpu.make_async_copy(
            held.at[slot], out_ref.at[:, pl.ds(pl.multiple_of(row, BLK), BLK), :], sems.at[slot]
        )

    def own_step(s, carry):
        left = zb_ref[pl.ds(pl.multiple_of(s * rows, rows), rows), :]
        prod = coupling_sq * jnp.dot(left, rhs[0], preferred_element_type=F32)
        for j in range(per_step):
            block = s * per_step + j
            row = pl.multiple_of(order_ref[box * face_blocks + block] * BLK, BLK)
            for part in range(2):
                piece = prod[j * BLK : (j + 1) * BLK, part * width : (part + 1) * width]
                held[block, part] = (
                    own_ref[part, pl.ds(row, BLK), :].astype(F32) * ext + piece
                ).astype(BF16)
            copy_out(block, parity, box * face_blocks, block).start()
        return carry

    def cross_step(s, carry):
        left = zs_ref[pl.ds(pl.multiple_of(s * rows, rows), rows), :]
        prod = -coupling * jnp.dot(left, rhs[1], preferred_element_type=F32)
        for j in range(per_step):
            block = s * per_step + j
            for part in range(2):
                piece = prod[j * BLK : (j + 1) * BLK, part * width : (part + 1) * width]
                held[face_blocks + block, part] = piece.astype(BF16)
            copy_out(face_blocks + block, 1 - parity, twin * face_blocks, block).start()
        return carry

    lax.fori_loop(0, steps, own_step, 0)
    lax.fori_loop(0, steps, cross_step, 0)

    def drain(block, carry):
        copy_out(block, parity, box * face_blocks, block).wait()
        copy_out(face_blocks + block, 1 - parity, twin * face_blocks, block).wait()
        return carry

    lax.fori_loop(0, face_blocks, drain, 0)


def shards(impedance, face_order):
    points, width = impedance.shape[3], impedance.shape[4]
    own = impedance.reshape(2, points, width)
    order = face_order.reshape(-1)
    face_blocks = points // BLK
    iface = MB * BLK
    n = lax.axis_size("grp")
    chunks = points // ROWS
    smem = pl.BlockSpec(memory_space=pltpu.SMEM)
    vmem = pl.BlockSpec(memory_space=pltpu.VMEM)
    z_shape = jax.ShapeDtypeStruct((points, 2 * iface), BF16)
    buffer = pltpu.VMEM((chunks, ROWS, 2 * iface), BF16)
    mine = pl.pallas_call(
        pick_kernel,
        out_shape=z_shape,
        in_specs=[smem, vmem],
        out_specs=vmem,
        compiler_params=pltpu.CompilerParams(vmem_limit_bytes=16 << 20),
    )(order, own)
    z_own, z_twin = pl.pallas_call(
        functools.partial(gather_kernel, n),
        out_shape=(z_shape, z_shape),
        in_specs=[vmem],
        out_specs=(vmem, vmem),
        scratch_shapes=[buffer] * 4 + [pltpu.SemaphoreType.DMA((chunks,))] * 6,
        compiler_params=pltpu.CompilerParams(
            collective_id=0, has_side_effects=True, vmem_limit_bytes=40 << 20
        ),
    )(mine)

    box = lax.axis_index("box")
    own_order = lax.dynamic_slice_in_dim(order, box * face_blocks, MB)
    col_blocks = (lax.axis_index("grp") * width + jnp.arange(width, dtype=jnp.int32)) // BLK
    on_face = jnp.any(col_blocks[None, :] == own_order[:, None], axis=0)
    ext = jnp.where(on_face, 0.0, 1.0).astype(F32)[None, :]

    rows = 4 * BLK
    merged = pl.pallas_call(
        functools.partial(product_kernel, rows),
        out_shape=jax.ShapeDtypeStruct((2, 2 * points, width), BF16),
        in_specs=[smem, vmem, vmem, vmem, vmem],
        out_specs=pl.BlockSpec(memory_space=pl.ANY),
        scratch_shapes=[
            pltpu.VMEM((2, 2 * iface, 2 * width), BF16),
            pltpu.VMEM((2 * iface, 2 * width), BF16),
            pltpu.VMEM((iface, 2 * width), F32),
            pltpu.VMEM((2 * face_blocks, 2, BLK, width), BF16),
            pltpu.SemaphoreType.DMA((2 * face_blocks,)),
        ],
        compiler_params=pltpu.CompilerParams(vmem_limit_bytes=48 << 20),
    )(order, own, z_own, z_twin, ext)
    return merged[:, None, None]


def solution(mesh):
    in_specs = (P(None, "box", None, None, "grp"), P())
    out_specs = P(None, "box", None, None, "grp")
    return jax.shard_map(shards, mesh=mesh, in_specs=in_specs, out_specs=out_specs, check_vma=False)
```

profile of v0, /device:TPU:1, one launch (start us, length us, event | category | flops | bytes accessed | tf_op | source)
XLA Modules:
  0.0 112.9 jit_solution(15781967984077333728)
XLA Ops:
  0.0 0.5 broadcast.60
  0.5 1.3 %reduce.3 = s32[8,16]{1,0:T(8,128)S(1)} reduce(s32[8,1,16]{2,1,0:T(1,128)} %param.3, s32[]{:T(128)} %broadcast.60), dimensions={1}, to_apply=%param.3.reduce_sub_computation.3 | reduce | bytes 1028 | tf_op args[1]
  1.9 0.1 reshape.36.order_ref
  2.0 0.1 dynamic_slice.3
  2.0 0.1 compare_reduce_fusion
  2.1 0.0 copy-start
  2.1 2.2 %copy-done = bf16[2,1,1,2048,512]{4,3,2,1,0:T(8,128)(2,1)S(1)} copy-done((bf16[2,1,1,2048,512]{4,3,2,1,0:T(8,128)(2,1)S(1)}, bf16[2,1,1,2048,512]{4,3,2,1,0:T(8,128)(2,1)}, u32[]{:S(2)}) %copy-start) | copy-done | bytes 4194328
  4.3 1.4 %shard_map.28.mine_ref = bf16[2048,768]{1,0:T(8,128)(2,1)S(1)} custom-call(s32[128]{0:T(128)S(1)} %reshape.36.order_ref, bf16[2,2048,512]{2,1,0:T(8,128)(2,1)S(1)} %bitcast.6), custom_call_target="tpu_custom_call" | custom-call | tf_op jit(solution)/shard_map/pallas_call | solution.py:262
  5.7 84.1 %shard_map.29 = (bf16[2048,768]{1,0:T(8,128)(2,1)S(1)}, bf16[2048,768]{1,0:T(8,128)(2,1)S(1)}) custom-call(bf16[2048,768]{1,0:T(8,128)(2,1)S(1)} %shard_map.28.mine_ref), custom_call_target="tpu_custom_call" | custom-call | tf_op jit(solution)/shard_map/pallas_call | solution.py:269
  89.8 0.0 copy-start.1
  89.8 1.7 %copy-done.1 = bf16[2048,768]{1,0:T(8,128)(2,1)} copy-done((bf16[2048,768]{1,0:T(8,128)(2,1)}, bf16[2048,768]{1,0:T(8,128)(2,1)S(1)}, u32[]{:S(2)}) %copy-start.1) | copy-done | bytes 3145752
  91.5 21.4 %shard_map.30 = bf16[2,4096,512]{2,1,0:T(8,128)(2,1)} custom-call(s32[128]{0:T(128)S(1)} %reshape.36.order_ref, bf16[2,2048,512]{2,1,0:T(8,128)(2,1)} %bitcast.5, bf16[2048,768]{1,0:T(8,128)(2,1)S(1)} %get-tuple-element.7.zb_ref, bf16[2048,768]{1,0:T(8,128)(2,1)} %copy-done.1, f32[1,512]{1,0:T(1,128)S(1)} %bitcast.7), custom_call_target="tpu_custom_call" | custom-call | tf_op jit(solution)/shard_map/pallas_call | solution.py:287
  (2 shorter events, 0.0 us)
Async XLA Ops:
  2.1 2.2 %copy-start = (bf16[2,1,1,2048,512]{4,3,2,1,0:T(8,128)(2,1)S(1)}, bf16[2,1,1,2048,512]{4,3,2,1,0:T(8,128)(2,1)}, u32[]{:S(2)}) copy-start(bf16[2,1,1,2048,512]{4,3,2,1,0:T(8,128)(2,1)} %param.2) | copy-start | bytes 12582916
  89.8 1.7 %copy-start.1 = (bf16[2048,768]{1,0:T(8,128)(2,1)}, bf16[2048,768]{1,0:T(8,128)(2,1)S(1)}, u32[]{:S(2)}) copy-start(bf16[2048,768]{1,0:T(8,128)(2,1)S(1)} %get-tuple-element.8.zs_ref) | copy-start | bytes 9437188
where the time goes:
time: 113 us
  Pallas kernels  107 us (95%)
  local copies, waits for them, and re-layouts  4.51 us (4%)
  other arithmetic  1.45 us (1%)
    pallas_call x1, Pallas kernels, shards(): pl.pallas_call(functools.partial(gather_kernel, n), out_shape=(z_shape, z...  84.1 us
    pallas_call x1, Pallas kernels, shards(): pl.pallas_call(functools.partial(product_kernel, rows), out_shape=jax.Sha...  21.4 us
    unnamed x5, local copies, waits for them, and re-layouts  4.36 us

commit v1 on v0

--- a/solution.py
+++ b/solution.py
@@ -17,10 +17,30 @@
 F32 = jnp.float32
 
 
-def pick_kernel(order_ref, own_ref, mine_ref):
+def exterior(order_ref, base, width):
+    blocks = width // BLK
+    first = lax.axis_index("grp") * blocks
+    pieces = []
+    for j in range(blocks):
+        keep = order_ref[base] != first + j
+        for k in range(1, MB):
+            keep = jnp.logical_and(keep, order_ref[base + k] != first + j)
+        pieces.append(jnp.full((1, BLK), keep.astype(F32), F32))
+    return jnp.concatenate(pieces, axis=1)
+
+
+def pick_kernel(order_ref, own_ref, mine_ref, rows_ref):
+    width = own_ref.shape[2]
     base = lax.axis_index("box") * (own_ref.shape[1] // BLK)
-    blocks = own_ref.shape[2] // BLK
+    blocks = width // BLK
     first = lax.axis_index("grp") * blocks
+    ext = exterior(order_ref, base, width)
+    for k in range(MB):
+        row = pl.multiple_of(order_ref[base + k] * BLK, BLK)
+        for part in range(2):
+            rows_ref[pl.ds(k * BLK, BLK), pl.ds(part * width, width)] = (
+                own_ref[part, pl.ds(row, BLK), :].astype(F32) * ext
+            ).astype(BF16)
 
     def body(block, carry):
         row = pl.multiple_of(order_ref[base + block] * BLK, BLK)
@@ -36,8 +56,16 @@
     lax.fori_loop(0, own_ref.shape[1] // BLK, body, 0)
 
 
+def put(dst, real, imag):
+    depth, width = real.shape
+    dst[pl.ds(0, depth), pl.ds(0, width)] = real
+    dst[pl.ds(0, depth), pl.ds(width, width)] = imag
+    dst[pl.ds(depth, depth), pl.ds(0, width)] = -imag
+    dst[pl.ds(depth, depth), pl.ds(width, width)] = real
+
+
 def gather_kernel(
-    n, mine_ref, zb_ref, zs_ref, buf_l, buf_r, out_r, out_l,
+    n, mine_ref, rows_ref, zb_ref, zs_ref, rhs_ref, high, low, buf_l, buf_r, out_r, out_l,
     send_r, recv_l, send_l, recv_r, send_t, recv_t,
 ):
     box = lax.axis_index("box")
@@ -116,6 +144,40 @@
         zb_ref[pl.ds(c * ROWS, ROWS), :] = out_r[c] + buf_r[c]
         to_twin(c).start()
 
+    points, width = zb_ref.shape[0], rows_ref.shape[1] // 2
+    coupling_sq = 1.0 / points
+    iface = MB * BLK
+
+    def split(value):
+        top = value.astype(BF16)
+        rest = (value - top.astype(F32)).astype(BF16)
+        put(high, top[:, :width], top[:, width:])
+        put(low, rest[:, :width], rest[:, width:])
+
+    def apply(z_ref):
+        left = z_ref[pl.ds(0, iface), :]
+        return jnp.dot(left, high[...], preferred_element_type=F32) + jnp.dot(
+            left, low[...], preferred_element_type=F32
+        )
+
+    face_chunks = iface // ROWS
+    stages = 2 * (2**NS_STEPS - 1)
+
+    def response_stage(stage):
+        if stage == 0:
+            for c in range(face_chunks):
+                to_twin(c).wait_recv()
+            put(high, rows_ref[:, :width], rows_ref[:, width:])
+            split(jnp.dot(zs_ref[pl.ds(0, iface), :], high[...], preferred_element_type=F32))
+        elif stage == stages:
+            rhs_ref[1] = high[...]
+            echoed = apply(zs_ref).astype(BF16)
+            put(rhs_ref.at[0], echoed[:, :width], echoed[:, width:])
+        elif stage % 2 == 1:
+            split(rows_ref[...].astype(F32) + coupling_sq * apply(zb_ref))
+        else:
+            split(apply(zs_ref))
+
     lag_l = LAG * grp
     lag_r = LAG * (n - 1 - grp)
     lag_f = jnp.maximum(lag_l, lag_r)
@@ -128,6 +190,12 @@
             def _():
                 step(c)
 
+        for stage in range(stages + 1):
+
+            @pl.when(t == lag_f + face_chunks + LAG + stage)
+            def _():
+                response_stage(stage)
+
         return carry
 
     lax.fori_loop(0, chunks + LAG * (n - 1), tick, 0)
@@ -142,65 +210,25 @@
             to_left(c).wait_send()
 
         to_twin(c).wait_send()
-        to_twin(c).wait_recv()
+
+        @pl.when(c >= face_chunks)
+        def _():
+            to_twin(c).wait_recv()
+
         return carry
 
     lax.fori_loop(0, chunks, drain, 0)
 
 
-def as_right_operand(pair):
-    real, imag = pair
-    return jnp.concatenate(
-        [jnp.concatenate([real, imag], axis=1), jnp.concatenate([-imag, real], axis=1)], axis=0
-    )
-
-
-def product_kernel(rows, order_ref, own_ref, zb_ref, zs_ref, ext_ref, out_ref, rhs, lo, base, held, sems):
+def product_kernel(rows, order_ref, own_ref, zb_ref, zs_ref, rhs, out_ref, held, sems):
     box = lax.axis_index("box")
     parity = lax.rem(box, 2)
     twin = box + 1 - 2 * parity
     points, width = own_ref.shape[1], own_ref.shape[2]
     face_blocks = points // BLK
-    iface = MB * BLK
     coupling_sq = 1.0 / points
     coupling = points ** (-0.5)
-    ext = ext_ref[...]
-
-    def put(dst, pair):
-        real, imag = pair
-        dst[pl.ds(0, iface), pl.ds(0, width)] = real
-        dst[pl.ds(0, iface), pl.ds(width, width)] = imag
-        dst[pl.ds(iface, iface), pl.ds(0, width)] = -imag
-        dst[pl.ds(iface, iface), pl.ds(width, width)] = real
-
-    def split(value):
-        high = value.astype(BF16)
-        low = (value - high.astype(F32)).astype(BF16)
-        put(rhs.at[0], (high[:, :width], high[:, width:]))
-        put(lo, (low[:, :width], low[:, width:]))
-
-    def apply(z_ref):
-        left = z_ref[pl.ds(0, iface), :]
-        return jnp.dot(left, rhs[0], preferred_element_type=F32) + jnp.dot(
-            left, lo[...], preferred_element_type=F32
-        )
-
-    for k in range(MB):
-        row = pl.multiple_of(order_ref[box * face_blocks + k] * BLK, BLK)
-        for part in range(2):
-            base[pl.ds(k * BLK, BLK), pl.ds(part * width, width)] = (
-                own_ref[part, pl.ds(row, BLK), :].astype(F32) * ext
-            )
-    split(base[...])
-    response = None
-    for _ in range(2**NS_STEPS - 1):
-        split(apply(zs_ref))
-        response = base[...] + coupling_sq * apply(zb_ref)
-        split(response)
-    echoed = apply(zs_ref).astype(BF16)
-    response = response.astype(BF16)
-    put(rhs.at[0], (echoed[:, :width], echoed[:, width:]))
-    put(rhs.at[1], (response[:, :width], response[:, width:]))
+    ext = exterior(order_ref, box * face_blocks, width)
 
     per_step = rows // BLK
     steps = points // rows
@@ -259,29 +287,24 @@
     vmem = pl.BlockSpec(memory_space=pltpu.VMEM)
     z_shape = jax.ShapeDtypeStruct((points, 2 * iface), BF16)
     buffer = pltpu.VMEM((chunks, ROWS, 2 * iface), BF16)
-    mine = pl.pallas_call(
+    mine, rows_in = pl.pallas_call(
         pick_kernel,
-        out_shape=z_shape,
+        out_shape=(z_shape, jax.ShapeDtypeStruct((iface, 2 * width), BF16)),
         in_specs=[smem, vmem],
-        out_specs=vmem,
+        out_specs=(vmem, vmem),
         compiler_params=pltpu.CompilerParams(vmem_limit_bytes=16 << 20),
     )(order, own)
-    z_own, z_twin = pl.pallas_call(
+    operand = pltpu.VMEM((2 * iface, 2 * width), BF16)
+    z_own, z_twin, rhs = pl.pallas_call(
         functools.partial(gather_kernel, n),
-        out_shape=(z_shape, z_shape),
-        in_specs=[vmem],
-        out_specs=(vmem, vmem),
-        scratch_shapes=[buffer] * 4 + [pltpu.SemaphoreType.DMA((chunks,))] * 6,
+        out_shape=(z_shape, z_shape, jax.ShapeDtypeStruct((2, 2 * iface, 2 * width), BF16)),
+        in_specs=[vmem, vmem],
+        out_specs=(vmem, vmem, vmem),
+        scratch_shapes=[operand] * 2 + [buffer] * 4 + [pltpu.SemaphoreType.DMA((chunks,))] * 6,
         compiler_params=pltpu.CompilerParams(
             collective_id=0, has_side_effects=True, vmem_limit_bytes=40 << 20
         ),
-    )(mine)
-
-    box = lax.axis_index("box")
-    own_order = lax.dynamic_slice_in_dim(order, box * face_blocks, MB)
-    col_blocks = (lax.axis_index("grp") * width + jnp.arange(width, dtype=jnp.int32)) // BLK
-    on_face = jnp.any(col_blocks[None, :] == own_order[:, None], axis=0)
-    ext = jnp.where(on_face, 0.0, 1.0).astype(F32)[None, :]
+    )(mine, rows_in)
 
     rows = 4 * BLK
     merged = pl.pallas_call(
@@ -290,14 +313,11 @@
         in_specs=[smem, vmem, vmem, vmem, vmem],
         out_specs=pl.BlockSpec(memory_space=pl.ANY),
         scratch_shapes=[
-            pltpu.VMEM((2, 2 * iface, 2 * width), BF16),
-            pltpu.VMEM((2 * iface, 2 * width), BF16),
-            pltpu.VMEM((iface, 2 * width), F32),
             pltpu.VMEM((2 * face_blocks, 2, BLK, width), BF16),
             pltpu.SemaphoreType.DMA((2 * face_blocks,)),
         ],
         compiler_params=pltpu.CompilerParams(vmem_limit_bytes=48 << 20),
-    )(order, own, z_own, z_twin, ext)
+    )(order, own, z_own, z_twin, rhs)
     return merged[:, None, None]
 
 

time: 113 us -> 107 us (0.947)
  Pallas kernels: 107 us -> 99.1 us
  local copies, waits for them, and re-layouts: 4.51 us -> 6.1 us
    pallas_call x1, Pallas kernels: 21.4 us -> 13.2 us  [shards(): pl.pallas_call(functools.partial(product_kernel, rows), out_shape=jax.Sha...]
    unnamed x5 -> x7, local copies, waits for them, and re-layouts: 4.36 us -> 6.02 us
where the time goes in v1:
time: 107 us
  Pallas kernels  99.1 us (93%)
  local copies, waits for them, and re-layouts  6.1 us (6%)
  other arithmetic  1.35 us (1%)
    pallas_call x1, Pallas kernels, shards(): pl.pallas_call(functools.partial(gather_kernel, n), out_shape=(z_shape, z...  84.4 us
    pallas_call x1, Pallas kernels, shards(): pl.pallas_call(functools.partial(product_kernel, rows), out_shape=jax.Sha...  13.2 us
    unnamed x7, local copies, waits for them, and re-layouts  6.02 us

profile of v1, /device:TPU:1, one launch (start us, length us, event | category | flops | bytes accessed | tf_op | source)
XLA Modules:
  0.0 106.6 jit_solution(14732752161967026798)
XLA Ops:
  0.0 0.5 broadcast.3
  0.5 1.3 %reduce.3 = s32[8,16]{1,0:T(8,128)S(1)} reduce(s32[8,1,16]{2,1,0:T(1,128)} %param.3, s32[]{:T(128)} %broadcast.3), dimensions={1}, to_apply=%param.3.reduce_sub_computation.3 | reduce | bytes 1028 | tf_op args[1]
  1.9 0.1 reshape.6.order_ref
  1.9 0.0 copy-start
  1.9 2.2 %copy-done = bf16[2,1,1,2048,512]{4,3,2,1,0:T(8,128)(2,1)S(1)} copy-done((bf16[2,1,1,2048,512]{4,3,2,1,0:T(8,128)(2,1)S(1)}, bf16[2,1,1,2048,512]{4,3,2,1,0:T(8,128)(2,1)}, u32[]{:S(2)}) %copy-start) | copy-done | bytes 4194328
  4.1 1.5 %shard_map.28 = (bf16[2048,768]{1,0:T(8,128)(2,1)S(1)}, bf16[384,1024]{1,0:T(8,128)(2,1)S(1)}) custom-call(s32[128]{0:T(128)S(1)} %reshape.6.order_ref, bf16[2,2048,512]{2,1,0:T(8,128)(2,1)S(1)} %bitcast.5), custom_call_target="tpu_custom_call" | custom-call | tf_op jit(solution)/shard_map/pallas_call | solution.py:290
  5.7 84.4 %shard_map.29 = (bf16[2048,768]{1,0:T(8,128)(2,1)S(1)}, bf16[2048,768]{1,0:T(8,128)(2,1)S(1)}, bf16[2,768,1024]{2,1,0:T(8,128)(2,1)S(1)}) custom-call(bf16[2048,768]{1,0:T(8,128)(2,1)S(1)} %get-tuple-element.10.mine_ref, bf16[384,1024]{1,0:T(8,128)(2,1)S(1)} %get-tuple-element.11.rows_ref), custom_call_target="tpu_custom_call" | custom-call | tf_op jit(solution)/shard_map/pallas_call | solution.py:298
  90.0 0.0 copy-start.1
  90.1 1.6 %copy-done.1 = bf16[2048,768]{1,0:T(8,128)(2,1)} copy-done((bf16[2048,768]{1,0:T(8,128)(2,1)}, bf16[2048,768]{1,0:T(8,128)(2,1)S(1)}, u32[]{:S(2)}) %copy-start.1) | copy-done | bytes 3145752
  91.7 0.0 copy-start.2
  91.7 1.7 %copy-done.2 = bf16[2,768,1024]{2,1,0:T(8,128)(2,1)} copy-done((bf16[2,768,1024]{2,1,0:T(8,128)(2,1)}, bf16[2,768,1024]{2,1,0:T(8,128)(2,1)S(1)}, u32[]{:S(2)}) %copy-start.2) | copy-done | bytes 3145752
  93.4 13.2 %shard_map.30 = bf16[2,4096,512]{2,1,0:T(8,128)(2,1)} custom-call(s32[128]{0:T(128)S(1)} %reshape.6.order_ref, bf16[2,2048,512]{2,1,0:T(8,128)(2,1)} %bitcast.4, bf16[2048,768]{1,0:T(8,128)(2,1)S(1)} %get-tuple-element.12.zb_ref, bf16[2048,768]{1,0:T(8,128)(2,1)} %copy-done.1, bf16[2,768,1024]{2,1,0:T(8,128)(2,1)} %copy-done.2), custom_call_target="tpu_custom_call" | custom-call | tf_op jit(solution)/shard_map/pallas_call | solution.py:310
Async XLA Ops:
  1.9 2.2 %copy-start = (bf16[2,1,1,2048,512]{4,3,2,1,0:T(8,128)(2,1)S(1)}, bf16[2,1,1,2048,512]{4,3,2,1,0:T(8,128)(2,1)}, u32[]{:S(2)}) copy-start(bf16[2,1,1,2048,512]{4,3,2,1,0:T(8,128)(2,1)} %param.2) | copy-start | bytes 12582916
  90.0 1.7 %copy-start.1 = (bf16[2048,768]{1,0:T(8,128)(2,1)}, bf16[2048,768]{1,0:T(8,128)(2,1)S(1)}, u32[]{:S(2)}) copy-start(bf16[2048,768]{1,0:T(8,128)(2,1)S(1)} %get-tuple-element.13.zs_ref) | copy-start | bytes 9437188
  91.7 1.7 %copy-start.2 = (bf16[2,768,1024]{2,1,0:T(8,128)(2,1)}, bf16[2,768,1024]{2,1,0:T(8,128)(2,1)S(1)}, u32[]{:S(2)}) copy-start(bf16[2,768,1024]{2,1,0:T(8,128)(2,1)S(1)} %get-tuple-element.14.rhs) | copy-start | bytes 9437188

commit v2 on v1

--- a/solution.py
+++ b/solution.py
@@ -34,13 +34,7 @@
     base = lax.axis_index("box") * (own_ref.shape[1] // BLK)
     blocks = width // BLK
     first = lax.axis_index("grp") * blocks
-    ext = exterior(order_ref, base, width)
-    for k in range(MB):
-        row = pl.multiple_of(order_ref[base + k] * BLK, BLK)
-        for part in range(2):
-            rows_ref[pl.ds(k * BLK, BLK), pl.ds(part * width, width)] = (
-                own_ref[part, pl.ds(row, BLK), :].astype(F32) * ext
-            ).astype(BF16)
+    ext = exterior(order_ref, base, width).astype(BF16)
 
     def body(block, carry):
         row = pl.multiple_of(order_ref[base + block] * BLK, BLK)
@@ -51,6 +45,10 @@
             for part in range(2):
                 piece = own_ref[part, pl.ds(row, BLK), pl.ds(col, BLK)]
                 mine_ref[pl.ds(block * BLK, BLK), pl.ds((part * MB + k) * BLK, BLK)] = piece * held
+        for part in range(2):
+            rows_ref[pl.ds(block * BLK, BLK), pl.ds(part * width, width)] = (
+                own_ref[part, pl.ds(row, BLK), :] * ext
+            )
         return carry
 
     lax.fori_loop(0, own_ref.shape[1] // BLK, body, 0)
@@ -65,7 +63,7 @@
 
 
 def gather_kernel(
-    n, mine_ref, rows_ref, zb_ref, zs_ref, rhs_ref, high, low, buf_l, buf_r, out_r, out_l,
+    n, mine_ref, rows_ref, own_out, cross_out, zb_ref, zs_ref, rhs_ref, high, low, buf_l, buf_r, out_r, out_l,
     send_r, recv_l, send_l, recv_r, send_t, recv_t,
 ):
     box = lax.axis_index("box")
@@ -146,6 +144,7 @@
 
     points, width = zb_ref.shape[0], rows_ref.shape[1] // 2
     coupling_sq = 1.0 / points
+    coupling = points ** (-0.5)
     iface = MB * BLK
 
     def split(value):
@@ -167,22 +166,42 @@
         if stage == 0:
             for c in range(face_chunks):
                 to_twin(c).wait_recv()
-            put(high, rows_ref[:, :width], rows_ref[:, width:])
+            put(high, rows_ref[pl.ds(0, iface), pl.ds(0, width)], rows_ref[pl.ds(0, iface), pl.ds(width, width)])
             split(jnp.dot(zs_ref[pl.ds(0, iface), :], high[...], preferred_element_type=F32))
         elif stage == stages:
             rhs_ref[1] = high[...]
             echoed = apply(zs_ref).astype(BF16)
             put(rhs_ref.at[0], echoed[:, :width], echoed[:, width:])
         elif stage % 2 == 1:
-            split(rows_ref[...].astype(F32) + coupling_sq * apply(zb_ref))
+            split(rows_ref[pl.ds(0, iface), :].astype(F32) + coupling_sq * apply(zb_ref))
         else:
             split(apply(zs_ref))
+
+    per_block = BLK // ROWS
+    blocks = points // BLK
+
+    def product_step(block):
+        for j in range(per_block):
+            c = block * per_block + j
+
+            @pl.when(c >= face_chunks)
+            def _():
+                to_twin(c).wait_recv()
+
+        rows = pl.ds(pl.multiple_of(block * BLK, BLK), BLK)
+        own = rows_ref[rows, :].astype(F32) + coupling_sq * jnp.dot(
+            zb_ref[rows, :], rhs_ref[0], preferred_element_type=F32
+        )
+        cross = -coupling * jnp.dot(zs_ref[rows, :], rhs_ref[1], preferred_element_type=F32)
+        for part in range(2):
+            own_out[block, part] = own[:, part * width : (part + 1) * width].astype(BF16)
+            cross_out[block, part] = cross[:, part * width : (part + 1) * width].astype(BF16)
 
     lag_l = LAG * grp
     lag_r = LAG * (n - 1 - grp)
     lag_f = jnp.maximum(lag_l, lag_r)
 
-    def tick(t, carry):
+    def tick(t, done):
         for lag, step in ((lag_l, left_step), (lag_r, right_step), (lag_f, full_step)):
             c = t - lag
 
@@ -196,9 +215,24 @@
             def _():
                 response_stage(stage)
 
+        ready = jnp.logical_and(
+            t > lag_f + face_chunks + LAG + stages, (done + 1) * per_block + LAG + lag_f <= t
+        )
+        ready = jnp.logical_and(ready, done < blocks)
+
+        @pl.when(ready)
+        def _():
+            product_step(done)
+
+        return done + ready.astype(jnp.int32)
+
+    done = lax.fori_loop(0, chunks + LAG * (n - 1), tick, jnp.int32(0))
+
+    def rest(block, carry):
+        product_step(block)
         return carry
 
-    lax.fori_loop(0, chunks + LAG * (n - 1), tick, 0)
+    lax.fori_loop(done, blocks, rest, 0)
 
     def drain(c, carry):
         @pl.when(has_right)
@@ -210,69 +244,29 @@
             to_left(c).wait_send()
 
         to_twin(c).wait_send()
-
-        @pl.when(c >= face_chunks)
-        def _():
-            to_twin(c).wait_recv()
-
         return carry
 
     lax.fori_loop(0, chunks, drain, 0)
 
 
-def product_kernel(rows, order_ref, own_ref, zb_ref, zs_ref, rhs, out_ref, held, sems):
+def place_kernel(order_ref, own_ref, cross_ref, out_ref, sems):
     box = lax.axis_index("box")
     parity = lax.rem(box, 2)
     twin = box + 1 - 2 * parity
-    points, width = own_ref.shape[1], own_ref.shape[2]
-    face_blocks = points // BLK
-    coupling_sq = 1.0 / points
-    coupling = points ** (-0.5)
-    ext = exterior(order_ref, box * face_blocks, width)
-
-    per_step = rows // BLK
-    steps = points // rows
-
-    def copy_out(slot, half, order_base, block):
-        row = half * points + order_ref[order_base + block] * BLK
-        return pltpu.make_async_copy(
-            held.at[slot], out_ref.at[:, pl.ds(pl.multiple_of(row, BLK), BLK), :], sems.at[slot]
-        )
-
-    def own_step(s, carry):
-        left = zb_ref[pl.ds(pl.multiple_of(s * rows, rows), rows), :]
-        prod = coupling_sq * jnp.dot(left, rhs[0], preferred_element_type=F32)
-        for j in range(per_step):
-            block = s * per_step + j
-            row = pl.multiple_of(order_ref[box * face_blocks + block] * BLK, BLK)
-            for part in range(2):
-                piece = prod[j * BLK : (j + 1) * BLK, part * width : (part + 1) * width]
-                held[block, part] = (
-                    own_ref[part, pl.ds(row, BLK), :].astype(F32) * ext + piece
-                ).astype(BF16)
-            copy_out(block, parity, box * face_blocks, block).start()
-        return carry
-
-    def cross_step(s, carry):
-        left = zs_ref[pl.ds(pl.multiple_of(s * rows, rows), rows), :]
-        prod = -coupling * jnp.dot(left, rhs[1], preferred_element_type=F32)
-        for j in range(per_step):
-            block = s * per_step + j
-            for part in range(2):
-                piece = prod[j * BLK : (j + 1) * BLK, part * width : (part + 1) * width]
-                held[face_blocks + block, part] = piece.astype(BF16)
-            copy_out(face_blocks + block, 1 - parity, twin * face_blocks, block).start()
-        return carry
-
-    lax.fori_loop(0, steps, own_step, 0)
-    lax.fori_loop(0, steps, cross_step, 0)
-
-    def drain(block, carry):
-        copy_out(block, parity, box * face_blocks, block).wait()
-        copy_out(face_blocks + block, 1 - parity, twin * face_blocks, block).wait()
-        return carry
-
-    lax.fori_loop(0, face_blocks, drain, 0)
+    blocks = own_ref.shape[0]
+    copies = []
+    for block in range(blocks):
+        for k, (src, half, order_base) in enumerate(
+            ((own_ref, parity, box * blocks), (cross_ref, 1 - parity, twin * blocks))
+        ):
+            row = pl.multiple_of((half * blocks + order_ref[order_base + block]) * BLK, BLK)
+            copy = pltpu.make_async_copy(
+                src.at[block], out_ref.at[:, pl.ds(row, BLK), :], sems.at[2 * block + k]
+            )
+            copy.start()
+            copies.append(copy)
+    for copy in copies:
+        copy.wait()
 
 
 def shards(impedance, face_order):
@@ -289,35 +283,35 @@
     buffer = pltpu.VMEM((chunks, ROWS, 2 * iface), BF16)
     mine, rows_in = pl.pallas_call(
         pick_kernel,
-        out_shape=(z_shape, jax.ShapeDtypeStruct((iface, 2 * width), BF16)),
+        out_shape=(z_shape, jax.ShapeDtypeStruct((points, 2 * width), BF16)),
         in_specs=[smem, vmem],
         out_specs=(vmem, vmem),
         compiler_params=pltpu.CompilerParams(vmem_limit_bytes=16 << 20),
     )(order, own)
     operand = pltpu.VMEM((2 * iface, 2 * width), BF16)
-    z_own, z_twin, rhs = pl.pallas_call(
+    out_shape = jax.ShapeDtypeStruct((face_blocks, 2, BLK, width), BF16)
+    own_out, cross_out = pl.pallas_call(
         functools.partial(gather_kernel, n),
-        out_shape=(z_shape, z_shape, jax.ShapeDtypeStruct((2, 2 * iface, 2 * width), BF16)),
+        out_shape=(out_shape, out_shape),
         in_specs=[vmem, vmem],
-        out_specs=(vmem, vmem, vmem),
-        scratch_shapes=[operand] * 2 + [buffer] * 4 + [pltpu.SemaphoreType.DMA((chunks,))] * 6,
+        out_specs=(vmem, vmem),
+        scratch_shapes=[pltpu.VMEM((points, 2 * iface), BF16)] * 2
+        + [pltpu.VMEM((2, 2 * iface, 2 * width), BF16)]
+        + [operand] * 2
+        + [buffer] * 4 + [pltpu.SemaphoreType.DMA((chunks,))] * 6,
         compiler_params=pltpu.CompilerParams(
-            collective_id=0, has_side_effects=True, vmem_limit_bytes=40 << 20
+            collective_id=0, has_side_effects=True, vmem_limit_bytes=36 << 20
         ),
     )(mine, rows_in)
 
-    rows = 4 * BLK
     merged = pl.pallas_call(
-        functools.partial(product_kernel, rows),
+        place_kernel,
         out_shape=jax.ShapeDtypeStruct((2, 2 * points, width), BF16),
-        in_specs=[smem, vmem, vmem, vmem, vmem],
+        in_specs=[smem, vmem, vmem],
         out_specs=pl.BlockSpec(memory_space=pl.ANY),
-        scratch_shapes=[
-            pltpu.VMEM((2 * face_blocks, 2, BLK, width), BF16),
-            pltpu.SemaphoreType.DMA((2 * face_blocks,)),
-        ],
-        compiler_params=pltpu.CompilerParams(vmem_limit_bytes=48 << 20),
-    )(order, own, z_own, z_twin, rhs)
+        scratch_shapes=[pltpu.SemaphoreType.DMA((2 * face_blocks,))],
+        compiler_params=pltpu.CompilerParams(vmem_limit_bytes=16 << 20),
+    )(order, own_out, cross_out)
     return merged[:, None, None]
 
 

time: 107 us -> 95.3 us (0.89)
  Pallas kernels: 99.1 us -> 90.9 us
  local copies, waits for them, and re-layouts: 6.1 us -> 2.78 us
    pallas_call x3, Pallas kernels: 99.1 us -> 90.9 us  [the longest x1 85.3 us: shards(): pl.pallas_call(functools.partial(gather_kernel, n), out_shape=(out_shape,...]
    unnamed x7 -> x3, local copies, waits for them, and re-layouts: 6.02 us -> 2.7 us
where the time goes in v2:
time: 95.3 us; the launch traced here: 95.1 us
  Pallas kernels  90.9 us (95%)
  local copies, waits for them, and re-layouts  2.78 us (3%)
  other arithmetic  1.35 us (1%)
    pallas_call x1, Pallas kernels, shards(): pl.pallas_call(functools.partial(gather_kernel, n), out_shape=(out_shape,...  85.3 us
    pallas_call x1, Pallas kernels, shards(): pl.pallas_call(place_kernel, out_shape=jax.ShapeDtypeStruct((2, 2 * point...  4.1 us
    unnamed x3, local copies, waits for them, and re-layouts  2.7 us

profile of v2, /device:TPU:1, one launch (start us, length us, event | category | flops | bytes accessed | tf_op | source)
XLA Modules:
  0.0 95.1 jit_solution(13642564049562702719)
XLA Ops:
  0.0 0.5 broadcast.3
  0.5 1.3 %reduce.3 = s32[8,16]{1,0:T(8,128)S(1)} reduce(s32[8,1,16]{2,1,0:T(1,128)} %param.3, s32[]{:T(128)} %broadcast.3), dimensions={1}, to_apply=%param.3.reduce_sub_computation.3 | reduce | bytes 1028 | tf_op args[1]
  1.9 0.1 reshape.6.order_ref
  1.9 0.0 copy-start
  1.9 2.2 %copy-done = bf16[2,1,1,2048,512]{4,3,2,1,0:T(8,128)(2,1)S(1)} copy-done((bf16[2,1,1,2048,512]{4,3,2,1,0:T(8,128)(2,1)S(1)}, bf16[2,1,1,2048,512]{4,3,2,1,0:T(8,128)(2,1)}, u32[]{:S(2)}) %copy-start) | copy-done | bytes 4194328
  4.1 1.6 %shard_map.28 = (bf16[2048,768]{1,0:T(8,128)(2,1)S(1)}, bf16[2048,1024]{1,0:T(8,128)(2,1)S(1)}) custom-call(s32[128]{0:T(128)S(1)} %reshape.6.order_ref, bf16[2,2048,512]{2,1,0:T(8,128)(2,1)S(1)} %bitcast.4), custom_call_target="tpu_custom_call" | custom-call | tf_op jit(solution)/shard_map/pallas_call | solution.py:284
  5.7 85.3 %shard_map.29 = (bf16[16,2,128,512]{3,2,1,0:T(8,128)(2,1)S(1)}, bf16[16,2,128,512]{3,2,1,0:T(8,128)(2,1)S(1)}) custom-call(bf16[2048,768]{1,0:T(8,128)(2,1)S(1)} %get-tuple-element.9.mine_ref, bf16[2048,1024]{1,0:T(8,128)(2,1)S(1)} %get-tuple-element.10.rows_ref), custom_call_target="tpu_custom_call" | custom-call | tf_op jit(solution)/shard_map/pallas_call | solution.py:293
  91.0 4.1 %shard_map.30 = bf16[2,4096,512]{2,1,0:T(8,128)(2,1)} custom-call(s32[128]{0:T(128)S(1)} %reshape.6.order_ref, bf16[16,2,128,512]{3,2,1,0:T(8,128)(2,1)S(1)} %get-tuple-element.11.own_ref, bf16[16,2,128,512]{3,2,1,0:T(8,128)(2,1)S(1)} %get-tuple-element.12.cross_ref), custom_call_target="tpu_custom_call" | custom-call | tf_op jit(solution)/shard_map/pallas_call | solution.py:307
Async XLA Ops:
  1.9 2.2 %copy-start = (bf16[2,1,1,2048,512]{4,3,2,1,0:T(8,128)(2,1)S(1)}, bf16[2,1,1,2048,512]{4,3,2,1,0:T(8,128)(2,1)}, u32[]{:S(2)}) copy-start(bf16[2,1,1,2048,512]{4,3,2,1,0:T(8,128)(2,1)} %param.2) | copy-start | bytes 12582916

commit v3 on v2

--- a/solution.py
+++ b/solution.py
@@ -10,8 +10,9 @@
 BLK = 128
 MB = 3
 NS_STEPS = 2
-ROWS = 64
+ROWS = 32
 LAG = 2
+STRIDE = 2
 MESH_ID = pl.DeviceIdType.MESH
 BF16 = jnp.bfloat16
 F32 = jnp.float32
@@ -22,24 +23,24 @@
     first = lax.axis_index("grp") * blocks
     pieces = []
     for j in range(blocks):
-        keep = order_ref[base] != first + j
+        keep = order_ref[base, 0, 0] != first + j
         for k in range(1, MB):
-            keep = jnp.logical_and(keep, order_ref[base + k] != first + j)
+            keep = jnp.logical_and(keep, order_ref[base, 0, k] != first + j)
         pieces.append(jnp.full((1, BLK), keep.astype(F32), F32))
     return jnp.concatenate(pieces, axis=1)
 
 
 def pick_kernel(order_ref, own_ref, mine_ref, rows_ref):
     width = own_ref.shape[2]
-    base = lax.axis_index("box") * (own_ref.shape[1] // BLK)
+    base = lax.axis_index("box")
     blocks = width // BLK
     first = lax.axis_index("grp") * blocks
     ext = exterior(order_ref, base, width).astype(BF16)
 
     def body(block, carry):
-        row = pl.multiple_of(order_ref[base + block] * BLK, BLK)
+        row = pl.multiple_of(order_ref[base, 0, block] * BLK, BLK)
         for k in range(MB):
-            local = order_ref[base + k] - first
+            local = order_ref[base, 0, k] - first
             held = jnp.logical_and(local >= 0, local < blocks).astype(F32).astype(BF16)
             col = pl.multiple_of(jnp.clip(local, 0, blocks - 1) * BLK, BLK)
             for part in range(2):
@@ -211,14 +212,14 @@
 
         for stage in range(stages + 1):
 
-            @pl.when(t == lag_f + face_chunks + LAG + stage)
+            @pl.when(t == lag_f + face_chunks + LAG + STRIDE * stage)
             def _():
                 response_stage(stage)
 
         ready = jnp.logical_and(
-            t > lag_f + face_chunks + LAG + stages, (done + 1) * per_block + LAG + lag_f <= t
-        )
-        ready = jnp.logical_and(ready, done < blocks)
+            t > lag_f + face_chunks + LAG + STRIDE * stages, (done + 1) * per_block + LAG + lag_f <= t
+        )
+        ready = jnp.logical_and(ready, jnp.logical_and(done < blocks, lax.rem(t, STRIDE) == 0))
 
         @pl.when(ready)
         def _():
@@ -257,9 +258,9 @@
     copies = []
     for block in range(blocks):
         for k, (src, half, order_base) in enumerate(
-            ((own_ref, parity, box * blocks), (cross_ref, 1 - parity, twin * blocks))
+            ((own_ref, parity, box), (cross_ref, 1 - parity, twin))
         ):
-            row = pl.multiple_of((half * blocks + order_ref[order_base + block]) * BLK, BLK)
+            row = pl.multiple_of((half * blocks + order_ref[order_base, 0, block]) * BLK, BLK)
             copy = pltpu.make_async_copy(
                 src.at[block], out_ref.at[:, pl.ds(row, BLK), :], sems.at[2 * block + k]
             )
@@ -272,7 +273,6 @@
 def shards(impedance, face_order):
     points, width = impedance.shape[3], impedance.shape[4]
     own = impedance.reshape(2, points, width)
-    order = face_order.reshape(-1)
     face_blocks = points // BLK
     iface = MB * BLK
     n = lax.axis_size("grp")
@@ -287,7 +287,7 @@
         in_specs=[smem, vmem],
         out_specs=(vmem, vmem),
         compiler_params=pltpu.CompilerParams(vmem_limit_bytes=16 << 20),
-    )(order, own)
+    )(face_order, own)
     operand = pltpu.VMEM((2 * iface, 2 * width), BF16)
     out_shape = jax.ShapeDtypeStruct((face_blocks, 2, BLK, width), BF16)
     own_out, cross_out = pl.pallas_call(
@@ -311,7 +311,7 @@
         out_specs=pl.BlockSpec(memory_space=pl.ANY),
         scratch_shapes=[pltpu.SemaphoreType.DMA((2 * face_blocks,))],
         compiler_params=pltpu.CompilerParams(vmem_limit_bytes=16 << 20),
-    )(order, own_out, cross_out)
+    )(face_order, own_out, cross_out)
     return merged[:, None, None]
 
 

time: 95.3 us -> 126 us (1.32)
  Pallas kernels: 90.9 us -> 123 us
  other arithmetic: 1.35 us -> 0 us
    pallas_call x1, Pallas kernels: 85.3 us -> 117 us  [shards(): pl.pallas_call(functools.partial(gather_kernel, n), out_shape=(out_shape,...]
    unnamed x1 -> x0, other arithmetic: 1.35 us -> none
    unnamed x3 -> x6, local copies, waits for them, and re-layouts: 2.7 us -> 2.88 us
where the time goes in v3:
time: 126 us
  Pallas kernels  123 us (98%)
  local copies, waits for them, and re-layouts  2.88 us (2%)
    pallas_call x1, Pallas kernels, shards(): pl.pallas_call(functools.partial(gather_kernel, n), out_shape=(out_shape,...  117 us
    pallas_call x1, Pallas kernels, shards(): pl.pallas_call(place_kernel, out_shape=jax.ShapeDtypeStruct((2, 2 * point...  4.15 us
    unnamed x6, local copies, waits for them, and re-layouts  2.88 us

profile of v3, /device:TPU:1, one launch (start us, length us, event | category | flops | bytes accessed | tf_op | source)
XLA Modules:
  0.0 126.0 jit_solution(17438402422357820280)
XLA Ops:
  0.0 0.0 copy-start
  0.0 2.2 %copy-done = bf16[2,1,1,2048,512]{4,3,2,1,0:T(8,128)(2,1)S(1)} copy-done((bf16[2,1,1,2048,512]{4,3,2,1,0:T(8,128)(2,1)S(1)}, bf16[2,1,1,2048,512]{4,3,2,1,0:T(8,128)(2,1)}, u32[]{:S(2)}) %copy-start) | copy-done | bytes 4194328
  2.2 0.0 copy-start.1
  2.2 0.7 copy-done.1
  2.9 1.6 %shard_map.28 = (bf16[2048,768]{1,0:T(8,128)(2,1)S(1)}, bf16[2048,1024]{1,0:T(8,128)(2,1)S(1)}) custom-call(s32[8,1,16]{2,1,0:T(1,128)S(1)} %copy-done.1, bf16[2,2048,512]{2,1,0:T(8,128)(2,1)S(1)} %bitcast.4), custom_call_target="tpu_custom_call" | custom-call | tf_op jit(solution)/shard_map/pallas_call | solution.py:284
  4.5 0.0 copy-start.2
  4.5 117.3 %shard_map.29 = (bf16[16,2,128,512]{3,2,1,0:T(8,128)(2,1)S(1)}, bf16[16,2,128,512]{3,2,1,0:T(8,128)(2,1)S(1)}) custom-call(bf16[2048,768]{1,0:T(8,128)(2,1)S(1)} %get-tuple-element.9.mine_ref, bf16[2048,1024]{1,0:T(8,128)(2,1)S(1)} %get-tuple-element.10.rows_ref), custom_call_target="tpu_custom_call" | custom-call | tf_op jit(solution)/shard_map/pallas_call | solution.py:293
  121.8 0.0 copy-done.2
  121.8 4.2 %shard_map.30 = bf16[2,4096,512]{2,1,0:T(8,128)(2,1)} custom-call(s32[8,1,16]{2,1,0:T(1,128)S(1)} %copy-done.2, bf16[16,2,128,512]{3,2,1,0:T(8,128)(2,1)S(1)} %get-tuple-element.11.own_ref, bf16[16,2,128,512]{3,2,1,0:T(8,128)(2,1)S(1)} %get-tuple-element.12.cross_ref), custom_call_target="tpu_custom_call" | custom-call | tf_op jit(solution)/shard_map/pallas_call | solution.py:307
Async XLA Ops:
  0.0 2.2 %copy-start = (bf16[2,1,1,2048,512]{4,3,2,1,0:T(8,128)(2,1)S(1)}, bf16[2,1,1,2048,512]{4,3,2,1,0:T(8,128)(2,1)}, u32[]{:S(2)}) copy-start(bf16[2,1,1,2048,512]{4,3,2,1,0:T(8,128)(2,1)} %param.2) | copy-start | bytes 12582916
  2.2 0.7 copy-start.1
  4.5 117.3 %copy-start.2 = (s32[8,1,16]{2,1,0:T(1,128)S(1)}, s32[8,1,16]{2,1,0:T(1,128)}, u32[]{:S(2)}) copy-start(s32[8,1,16]{2,1,0:T(1,128)} %order_ref.3) | copy-start | bytes 1540

commit v4 on v3

--- a/solution.py
+++ b/solution.py
@@ -10,9 +10,9 @@
 BLK = 128
 MB = 3
 NS_STEPS = 2
-ROWS = 32
+ROWS = 64
 LAG = 2
-STRIDE = 2
+STRIDE = 1
 MESH_ID = pl.DeviceIdType.MESH
 BF16 = jnp.bfloat16
 F32 = jnp.float32

time: 126 us -> 94.1 us (0.75)
  Pallas kernels: 123 us -> 91 us
    pallas_call x1, Pallas kernels: 117 us -> 85.2 us  [shards(): pl.pallas_call(functools.partial(gather_kernel, n), out_shape=(out_shape,...]
where the time goes in v4:
time: 94.1 us; the launch traced here: 93.9 us
  Pallas kernels  91 us (97%)
  local copies, waits for them, and re-layouts  2.88 us (3%)
    pallas_call x1, Pallas kernels, shards(): pl.pallas_call(functools.partial(gather_kernel, n), out_shape=(out_shape,...  85.2 us
    pallas_call x1, Pallas kernels, shards(): pl.pallas_call(place_kernel, out_shape=jax.ShapeDtypeStruct((2, 2 * point...  4.15 us
    unnamed x6, local copies, waits for them, and re-layouts  2.88 us

profile of v4, /device:TPU:1, one launch (start us, length us, event | category | flops | bytes accessed | tf_op | source)
XLA Modules:
  0.0 93.9 jit_solution(13428787028616300384)
XLA Ops:
  0.0 0.0 copy-start
  0.0 2.2 %copy-done = bf16[2,1,1,2048,512]{4,3,2,1,0:T(8,128)(2,1)S(1)} copy-done((bf16[2,1,1,2048,512]{4,3,2,1,0:T(8,128)(2,1)S(1)}, bf16[2,1,1,2048,512]{4,3,2,1,0:T(8,128)(2,1)}, u32[]{:S(2)}) %copy-start) | copy-done | bytes 4194328
  2.2 0.0 copy-start.1
  2.2 0.7 copy-done.1
  2.9 1.6 %shard_map.28 = (bf16[2048,768]{1,0:T(8,128)(2,1)S(1)}, bf16[2048,1024]{1,0:T(8,128)(2,1)S(1)}) custom-call(s32[8,1,16]{2,1,0:T(1,128)S(1)} %copy-done.1, bf16[2,2048,512]{2,1,0:T(8,128)(2,1)S(1)} %bitcast.4), custom_call_target="tpu_custom_call" | custom-call | tf_op jit(solution)/shard_map/pallas_call | solution.py:284
  4.5 0.0 copy-start.2
  4.5 85.2 %shard_map.29 = (bf16[16,2,128,512]{3,2,1,0:T(8,128)(2,1)S(1)}, bf16[16,2,128,512]{3,2,1,0:T(8,128)(2,1)S(1)}) custom-call(bf16[2048,768]{1,0:T(8,128)(2,1)S(1)} %get-tuple-element.9.mine_ref, bf16[2048,1024]{1,0:T(8,128)(2,1)S(1)} %get-tuple-element.10.rows_ref), custom_call_target="tpu_custom_call" | custom-call | tf_op jit(solution)/shard_map/pallas_call | solution.py:293
  89.8 0.0 copy-done.2
  89.8 4.2 %shard_map.30 = bf16[2,4096,512]{2,1,0:T(8,128)(2,1)} custom-call(s32[8,1,16]{2,1,0:T(1,128)S(1)} %copy-done.2, bf16[16,2,128,512]{3,2,1,0:T(8,128)(2,1)S(1)} %get-tuple-element.11.own_ref, bf16[16,2,128,512]{3,2,1,0:T(8,128)(2,1)S(1)} %get-tuple-element.12.cross_ref), custom_call_target="tpu_custom_call" | custom-call | tf_op jit(solution)/shard_map/pallas_call | solution.py:307
Async XLA Ops:
  0.0 2.2 %copy-start = (bf16[2,1,1,2048,512]{4,3,2,1,0:T(8,128)(2,1)S(1)}, bf16[2,1,1,2048,512]{4,3,2,1,0:T(8,128)(2,1)}, u32[]{:S(2)}) copy-start(bf16[2,1,1,2048,512]{4,3,2,1,0:T(8,128)(2,1)} %param.2) | copy-start | bytes 12582916
  2.2 0.7 copy-start.1
  4.5 85.2 %copy-start.2 = (s32[8,1,16]{2,1,0:T(1,128)S(1)}, s32[8,1,16]{2,1,0:T(1,128)}, u32[]{:S(2)}) copy-start(s32[8,1,16]{2,1,0:T(1,128)} %order_ref.3) | copy-start | bytes 1540

commit v5 on v3

--- a/solution.py
+++ b/solution.py
@@ -11,7 +11,7 @@
 MB = 3
 NS_STEPS = 2
 ROWS = 32
-LAG = 2
+LAG = 3
 STRIDE = 2
 MESH_ID = pl.DeviceIdType.MESH
 BF16 = jnp.bfloat16

time: 126 us -> 100 us (0.79)
  Pallas kernels: 123 us -> 97.3 us
    pallas_call x1, Pallas kernels: 117 us -> 91.6 us  [shards(): pl.pallas_call(functools.partial(gather_kernel, n), out_shape=(out_shape,...]
where the time goes in v5:
time: 100 us
  Pallas kernels  97.3 us (97%)
  local copies, waits for them, and re-layouts  2.88 us (3%)
    pallas_call x1, Pallas kernels, shards(): pl.pallas_call(functools.partial(gather_kernel, n), out_shape=(out_shape,...  91.6 us
    pallas_call x1, Pallas kernels, shards(): pl.pallas_call(place_kernel, out_shape=jax.ShapeDtypeStruct((2, 2 * point...  4.15 us
    unnamed x6, local copies, waits for them, and re-layouts  2.88 us

profile of v5, /device:TPU:1, one launch (start us, length us, event | category | flops | bytes accessed | tf_op | source)
XLA Modules:
  0.0 100.3 jit_solution(8004266983399830892)
XLA Ops:
  0.0 0.0 copy-start
  0.0 2.2 %copy-done = bf16[2,1,1,2048,512]{4,3,2,1,0:T(8,128)(2,1)S(1)} copy-done((bf16[2,1,1,2048,512]{4,3,2,1,0:T(8,128)(2,1)S(1)}, bf16[2,1,1,2048,512]{4,3,2,1,0:T(8,128)(2,1)}, u32[]{:S(2)}) %copy-start) | copy-done | bytes 4194328
  2.2 0.0 copy-start.1
  2.2 0.7 copy-done.1
  2.9 1.6 %shard_map.28 = (bf16[2048,768]{1,0:T(8,128)(2,1)S(1)}, bf16[2048,1024]{1,0:T(8,128)(2,1)S(1)}) custom-call(s32[8,1,16]{2,1,0:T(1,128)S(1)} %copy-done.1, bf16[2,2048,512]{2,1,0:T(8,128)(2,1)S(1)} %bitcast.4), custom_call_target="tpu_custom_call" | custom-call | tf_op jit(solution)/shard_map/pallas_call | solution.py:284
  4.5 0.0 copy-start.2
  4.5 91.6 %shard_map.29 = (bf16[16,2,128,512]{3,2,1,0:T(8,128)(2,1)S(1)}, bf16[16,2,128,512]{3,2,1,0:T(8,128)(2,1)S(1)}) custom-call(bf16[2048,768]{1,0:T(8,128)(2,1)S(1)} %get-tuple-element.9.mine_ref, bf16[2048,1024]{1,0:T(8,128)(2,1)S(1)} %get-tuple-element.10.rows_ref), custom_call_target="tpu_custom_call" | custom-call | tf_op jit(solution)/shard_map/pallas_call | solution.py:293
  96.1 0.0 copy-done.2
  96.1 4.2 %shard_map.30 = bf16[2,4096,512]{2,1,0:T(8,128)(2,1)} custom-call(s32[8,1,16]{2,1,0:T(1,128)S(1)} %copy-done.2, bf16[16,2,128,512]{3,2,1,0:T(8,128)(2,1)S(1)} %get-tuple-element.11.own_ref, bf16[16,2,128,512]{3,2,1,0:T(8,128)(2,1)S(1)} %get-tuple-element.12.cross_ref), custom_call_target="tpu_custom_call" | custom-call | tf_op jit(solution)/shard_map/pallas_call | solution.py:307
Async XLA Ops:
  0.0 2.2 %copy-start = (bf16[2,1,1,2048,512]{4,3,2,1,0:T(8,128)(2,1)S(1)}, bf16[2,1,1,2048,512]{4,3,2,1,0:T(8,128)(2,1)}, u32[]{:S(2)}) copy-start(bf16[2,1,1,2048,512]{4,3,2,1,0:T(8,128)(2,1)} %param.2) | copy-start | bytes 12582916
  2.2 0.7 copy-start.1
  4.5 91.6 %copy-start.2 = (s32[8,1,16]{2,1,0:T(1,128)S(1)}, s32[8,1,16]{2,1,0:T(1,128)}, u32[]{:S(2)}) copy-start(s32[8,1,16]{2,1,0:T(1,128)} %order_ref.3) | copy-start | bytes 1540
